TPU v7x, 32 devices: a whole 2x2x4 slice. The times are simulated.
32 devices in a mesh: expert: 8 (over z, y), hidden: 4 (over x, core).
Axes of the slice: x: 2, y: 2, z: 4, core: 2. Of those that a mesh axis runs over, the one named last changes fastest.
Arguments:
- tokens: bfloat16 [512, 7168], P('expert'), may hold values from -6 to 6
- expert_ids: int32 [512, 8], replicated, may hold values from 0 to 31, all different within a row; in each aligned block of 64 rows (0 to 63, 64 to 127, ...) at most 24 rows name the same one
- gate_weight: bfloat16 [32, 7168, 2048], P('expert', None, 'hidden')
- up_weight: bfloat16 [32, 7168, 2048], P('expert', None, 'hidden')
Outputs:
- expert_hidden: bfloat16 [32, 8, 24, 2048], P('expert', None, None, 'hidden')
Inputs may be any that keep to these rules, and one draw needn't show every extreme that they name: `expert_ids`: each row names 8 different experts; among the rows of one device no expert is named more than 24 times, and in every draw some expert is named exactly 24 times there.
All inputs are finite; a program needn't handle non-finite values.
Results may differ from a plain program's by a relative error of at most 0.0058.
Values may be sent and summed in bfloat16 or wider, within the bound.
A program may use at most 192 MiB of HBM per device.

v0:
```python
import jax
import jax.numpy as jnp
from jax import lax
from jax.sharding import PartitionSpec as P

TOPK = 8
EXPERTS = 32
SWEEPS = 5
TOK_DEV = 64
CAP = 24


EPS = 1e-06


def slot_table(block_ids):
    flat_ids = block_ids.reshape(-1)
    onehot = (flat_ids[:, None] == jnp.arange(EXPERTS, dtype=jnp.int32)[None, :]).astype(jnp.int32)
    before = jnp.cumsum(onehot, axis=0) - onehot
    my_rank = jnp.sum(before * onehot, axis=1)
    token_index = jnp.arange(flat_ids.shape[0], dtype=jnp.int32) // TOPK
    position = flat_ids * CAP + my_rank
    filled = jnp.full((EXPERTS * CAP,), TOK_DEV, jnp.int32).at[position].set(token_index)
    return filled.reshape(EXPERTS, CAP)


def row_terms(weight, cols_sq):
    values = weight.astype(jnp.float32)
    return jnp.sum(values * values * cols_sq[:, None, :], axis=2)


def col_terms(weight, scale_sq):
    values = weight.astype(jnp.float32)
    return jnp.sum(values * values * scale_sq[:, :, None], axis=1)


def shards(tokens, expert_ids, gate_weight, up_weight):
    exp_local = gate_weight.shape[0]
    width = gate_weight.shape[1]
    ff_local = gate_weight.shape[2]
    ff_total = ff_local * lax.axis_size("hidden")
    my_index = lax.axis_index("expert")
    gate_cols = jnp.ones((exp_local, ff_local), jnp.float32)
    up_cols = jnp.ones((exp_local, ff_local), jnp.float32)
    for sweep in range(SWEEPS):
        partial_rows = row_terms(gate_weight, gate_cols * gate_cols) + row_terms(
            up_weight, up_cols * up_cols
        )
        row_sums = lax.psum(partial_rows, "hidden")
        row_scale = lax.rsqrt(width * row_sums / (2 * ff_total) + EPS)
        scale_sq = row_scale * row_scale
        gate_cols = lax.rsqrt(col_terms(gate_weight, scale_sq) + EPS)
        up_cols = lax.rsqrt(col_terms(up_weight, scale_sq) + EPS)
    gate_eq = (
        gate_weight.astype(jnp.float32) * row_scale[:, :, None] * gate_cols[:, None, :]
    ).astype(jnp.bfloat16)
    up_eq = (up_weight.astype(jnp.float32) * row_scale[:, :, None] * up_cols[:, None, :]).astype(
        jnp.bfloat16
    )
    tok_local = tokens.shape[0]
    padded = jnp.concatenate([tokens, jnp.zeros((1, width), jnp.bfloat16)], axis=0)
    block_ids = lax.dynamic_slice_in_dim(expert_ids, my_index * tok_local, tok_local, 0)
    slot_index = slot_table(block_ids)
    outgoing = padded[slot_index.reshape(-1)].reshape(EXPERTS, 1, CAP, width)
    routed = lax.all_to_all(outgoing, "expert", split_axis=0, concat_axis=1, tiled=True)
    gate_act = jnp.einsum("ensd,edf->ensf", routed, gate_eq, preferred_element_type=jnp.float32)
    up_act = jnp.einsum("ensd,edf->ensf", routed, up_eq, preferred_element_type=jnp.float32)
    return (jax.nn.silu(gate_act) * up_act).astype(jnp.bfloat16)


def solution(mesh):
    in_specs = (P("expert", None), P(), P("expert", None, "hidden"), P("expert", None, "hidden"))
    out_specs = P("expert", None, None, "hidden")
    return jax.shard_map(shards, mesh=mesh, in_specs=in_specs, out_specs=out_specs, check_vma=False)
```

profile of v0, /device:TPU:0, one launch (start us, length us, event | category | flops | bytes accessed | tf_op | source)
XLA Modules:
  0.0 466.9 jit_solution(1450112305214453791)
XLA Ops:
  6.5 19.0 %fusion.9 = (f32[4,7168]{1,0:T(4,128)S(1)}, f32[4,7168]{1,0:T(4,128)S(1)}) fusion(bf16[4,7168,512]{2,1,0:T(8,128)(2,1)} %param.7, bf16[4,7168,512]{2,1,0:T(8,128)(2,1)} %param.6), kind=kLoop, calls=%fused_computation.13 | loop fusion | flops 88023040 | bytes 58949632 | tf_op jit(solution)/shard_map/reduce_sum | solution.py:29
  26.3 0.8 broadcast_multiply_fusion
  27.5 1.2 reduce-window.6
  29.1 2.4 scatter_custom_fusion
  31.6 27.5 %all-reduce.7.cloned.1.call-done = f32[4,7168]{1,0:T(4,128)} async-done(((f32[4,7168]{1,0:T(4,128)}), f32[4,7168]{1,0:T(4,128)}) %all-reduce.7.cloned.1.call-update) | async-done | bytes 114704 | tf_op jit(solution)/shard_map/psum | solution.py:49
  59.1 0.9 rsqrt_multiply_fusion.3
  60.1 19.2 %fusion.31 = (f32[4,512]{1,0:T(4,128)S(1)}, f32[4,512]{1,0:T(4,128)S(1)}) fusion(bf16[4,7168,512]{2,1,0:T(8,128)(2,1)} %param.7, f32[4,7168]{1,0:T(4,128)S(1)} %rsqrt_multiply_fusion.3, bf16[4,7168,512]{2,1,0:T(8,128)(2,1)} %param.6), kind=kLoop, calls=%fused_computation.37 | loop fusion | flops 117436416 | bytes 58851328 | tf_op jit(solution)/shard_map/reduce_sum | solution.py:34
  79.3 10.7 %fusion.21 = f32[4,7168]{1,0:T(4,128)S(1)} fusion(bf16[4,7168,512]{2,1,0:T(8,128)(2,1)} %param.6, f32[4,512]{1,0:T(4,128)S(1)} %rsqrt_multiply_fusion.11), kind=kLoop, calls=%fused_computation.27 | loop fusion | flops 58691584 | bytes 29483008 | tf_op jit(solution)/shard_map/reduce_sum | solution.py:29
  90.0 10.6 %fusion.32 = f32[4,7168]{1,0:T(4,128)S(1)} fusion(bf16[4,7168,512]{2,1,0:T(8,128)(2,1)} %param.7, f32[4,512]{1,0:T(4,128)S(1)} %rsqrt_multiply_fusion.10), kind=kLoop, calls=%fused_computation.38 | loop fusion | flops 58691584 | bytes 29483008 | tf_op jit(solution)/shard_map/reduce_sum | solution.py:29
  101.4 31.4 %all-reduce.9.cloned.1.call-done = f32[4,7168]{1,0:T(4,128)} async-done(((f32[4,7168]{1,0:T(4,128)}), f32[4,7168]{1,0:T(4,128)}) %all-reduce.9.cloned.1.call-update) | async-done | bytes 114704 | tf_op jit(solution)/shard_map/psum | solution.py:49
  132.8 0.9 rsqrt_multiply_fusion.2
  133.7 19.2 %fusion.33 = (f32[4,512]{1,0:T(4,128)S(1)}, f32[4,512]{1,0:T(4,128)S(1)}) fusion(bf16[4,7168,512]{2,1,0:T(8,128)(2,1)} %param.7, f32[4,7168]{1,0:T(4,128)S(1)} %rsqrt_multiply_fusion.2, bf16[4,7168,512]{2,1,0:T(8,128)(2,1)} %param.6), kind=kLoop, calls=%fused_computation.39 | loop fusion | flops 117436416 | bytes 58851328 | tf_op jit(solution)/shard_map/reduce_sum | solution.py:34
  152.9 10.6 %fusion.23 = f32[4,7168]{1,0:T(4,128)S(1)} fusion(bf16[4,7168,512]{2,1,0:T(8,128)(2,1)} %param.6, f32[4,512]{1,0:T(4,128)S(1)} %rsqrt_multiply_fusion.9), kind=kLoop, calls=%fused_computation.29 | loop fusion | flops 58691584 | bytes 29483008 | tf_op jit(solution)/shard_map/reduce_sum | solution.py:29
  163.5 10.6 %fusion.34 = f32[4,7168]{1,0:T(4,128)S(1)} fusion(bf16[4,7168,512]{2,1,0:T(8,128)(2,1)} %param.7, f32[4,512]{1,0:T(4,128)S(1)} %rsqrt_multiply_fusion.8), kind=kLoop, calls=%fused_computation.40 | loop fusion | flops 58691584 | bytes 29483008 | tf_op jit(solution)/shard_map/reduce_sum | solution.py:29
  174.8 9.4 %gather_fusion = bf16[768,7168]{1,0:T(8,128)(2,1)} fusion(bf16[65,7168]{1,0:T(8,128)(2,1)S(1)} %concatenate.3, s32[1024]{0:T(1024)S(1)} %pad_clamp_fusion), kind=kCustom, calls=%fused_computation | custom fusion | bytes 22023168 | tf_op jit(solution)/shard_map/gather | solution.py:64
  184.2 5.5 %all-to-all-start = ((bf16[32,1,24,7168]{3,2,1,0:T(8,128)(2,1)}), bf16[32,1,24,7168]{3,2,1,0:T(8,128)(2,1)}, u32[]{:S(2)}, u32[]{:S(2)}) async-start(bf16[32,1,24,7168]{3,2,1,0:T(8,128)(2,1)} %bitcast.47), calls=%async_computation | async-start | bytes 22020096 | tf_op jit(solution)/shard_map/all_to_all | solution.py:65
  190.0 16.4 %all-reduce.11.cloned.1.call-done = f32[4,7168]{1,0:T(4,128)} async-done(((f32[4,7168]{1,0:T(4,128)}), f32[4,7168]{1,0:T(4,128)}) %all-reduce.11.cloned.1.call-update) | async-done | bytes 114704 | tf_op jit(solution)/shard_map/psum | solution.py:49
  206.3 0.9 rsqrt_multiply_fusion.1
  207.3 19.2 %fusion.35 = (f32[4,512]{1,0:T(4,128)S(1)}, f32[4,512]{1,0:T(4,128)S(1)}) fusion(bf16[4,7168,512]{2,1,0:T(8,128)(2,1)} %param.7, f32[4,7168]{1,0:T(4,128)S(1)} %rsqrt_multiply_fusion.1, bf16[4,7168,512]{2,1,0:T(8,128)(2,1)} %param.6), kind=kLoop, calls=%fused_computation.41 | loop fusion | flops 117436416 | bytes 58851328 | tf_op jit(solution)/shard_map/reduce_sum | solution.py:34
  226.5 10.6 %fusion.25 = f32[4,7168]{1,0:T(4,128)S(1)} fusion(bf16[4,7168,512]{2,1,0:T(8,128)(2,1)} %param.6, f32[4,512]{1,0:T(4,128)S(1)} %rsqrt_multiply_fusion.7), kind=kLoop, calls=%fused_computation.31 | loop fusion | flops 58691584 | bytes 29483008 | tf_op jit(solution)/shard_map/reduce_sum | solution.py:29
  237.1 10.6 %fusion.36 = f32[4,7168]{1,0:T(4,128)S(1)} fusion(bf16[4,7168,512]{2,1,0:T(8,128)(2,1)} %param.7, f32[4,512]{1,0:T(4,128)S(1)} %rsqrt_multiply_fusion.6), kind=kLoop, calls=%fused_computation.42 | loop fusion | flops 58691584 | bytes 29483008 | tf_op jit(solution)/shard_map/reduce_sum | solution.py:29
  248.4 31.5 %all-reduce.13.cloned.1.call-done = f32[4,7168]{1,0:T(4,128)} async-done(((f32[4,7168]{1,0:T(4,128)}), f32[4,7168]{1,0:T(4,128)}) %all-reduce.13.cloned.1.call-update) | async-done | bytes 114704 | tf_op jit(solution)/shard_map/psum | solution.py:49
  279.9 0.9 rsqrt_multiply_fusion
  280.8 19.2 %fusion.37 = (f32[4,512]{1,0:T(4,128)S(1)}, f32[4,512]{1,0:T(4,128)S(1)}) fusion(bf16[4,7168,512]{2,1,0:T(8,128)(2,1)} %param.7, f32[4,7168]{1,0:T(4,128)S(1)} %rsqrt_multiply_fusion, bf16[4,7168,512]{2,1,0:T(8,128)(2,1)} %param.6), kind=kLoop, calls=%fused_computation.43 | loop fusion | flops 117436416 | bytes 58851328 | tf_op jit(solution)/shard_map/reduce_sum | solution.py:34
  300.0 10.6 %fusion.27 = f32[4,7168]{1,0:T(4,128)S(1)} fusion(bf16[4,7168,512]{2,1,0:T(8,128)(2,1)} %param.6, f32[4,512]{1,0:T(4,128)S(1)} %rsqrt_multiply_fusion.5), kind=kLoop, calls=%fused_computation.33 | loop fusion | flops 58691584 | bytes 29483008 | tf_op jit(solution)/shard_map/reduce_sum | solution.py:29
  310.6 10.6 %fusion.38 = f32[4,7168]{1,0:T(4,128)S(1)} fusion(bf16[4,7168,512]{2,1,0:T(8,128)(2,1)} %param.7, f32[4,512]{1,0:T(4,128)S(1)} %rsqrt_multiply_fusion.4), kind=kLoop, calls=%fused_computation.44 | loop fusion | flops 58691584 | bytes 29483008 | tf_op jit(solution)/shard_map/reduce_sum | solution.py:29
  321.9 31.5 %all-reduce.15.cloned.1.call-done = f32[4,7168]{1,0:T(4,128)} async-done(((f32[4,7168]{1,0:T(4,128)}), f32[4,7168]{1,0:T(4,128)}) %all-reduce.15.cloned.1.call-update) | async-done | bytes 114704 | tf_op jit(solution)/shard_map/psum | solution.py:49
  353.4 0.9 add_rsqrt_fusion
  354.4 19.2 %fusion.28 = (f32[4,512]{1,0:T(4,128)S(1)}, f32[4,512]{1,0:T(4,128)S(1)}) fusion(bf16[4,7168,512]{2,1,0:T(8,128)(2,1)} %param.6, f32[4,7168]{1,0:T(4,128)S(1)} %get-tuple-element.18, bf16[4,7168,512]{2,1,0:T(8,128)(2,1)} %param.7), kind=kLoop, calls=%fused_computation.34 | loop fusion | flops 117436416 | bytes 58851328 | tf_op jit(solution)/shard_map/reduce_sum | solution.py:34
  373.6 55.9 %all-to-all-done = bf16[32,1,24,7168]{3,2,1,0:T(8,128)(2,1)} async-done(((bf16[32,1,24,7168]{3,2,1,0:T(8,128)(2,1)}), bf16[32,1,24,7168]{3,2,1,0:T(8,128)(2,1)}, u32[]{:S(2)}, u32[]{:S(2)}) %all-to-all-start) | async-done | bytes 11010080 | tf_op jit(solution)/shard_map/all_to_all | solution.py:65
  429.5 15.0 %fusion.46 = f32[4,8,24,512]{3,2,1,0:T(8,128)S(1)} fusion(bf16[4,7168,512]{2,1,0:T(8,128)(2,1)} %param.7, f32[4,512]{1,0:T(4,128)S(1)} %add_rsqrt_fusion.1, f32[4,7168]{1,0:T(4,128)S(1)} %get-tuple-element.17, bf16[8,4,1,24,7168]{4,3,1,0,2:T(8,128)(2,1)} %bitcast.5), kind=kOutput, calls=%fused_computation.51 | convolution fusion | flops 5695864832 | bytes 42065920 | tf_op jit(solution)/shard_map/ensd,edf->ensf/dot_general | solution.py:67
  444.5 15.9 %multiply_convert_fusion = bf16[4,8,24,512]{3,2,1,0:T(8,128)(2,1)} fusion(f32[4,8,24,512]{3,2,1,0:T(8,128)S(1)} %fusion.46, bf16[4,7168,512]{2,1,0:T(8,128)(2,1)} %param.6, f32[4,512]{1,0:T(4,128)S(1)} %add_rsqrt_fusion.2, f32[4,7168]{1,0:T(4,128)S(1)} %get-tuple-element.17, bf16[8,4,1,24,7168]{4,3,1,0,2:T(8,128)(2,1)} %bitcast.5), kind=kOutput, calls=%fused_computation.56 | convolution fusion | flops 5698224128 | bytes 42852352 | tf_op jit(solution)/shard_map/ensd,edf->ensf/dot_general | solution.py:66
  (42 shorter events, 4.8 us)
Async XLA Ops:
  6.5 52.6 %all-reduce.7.cloned.1.call-start = ((), (), s32[]{:S(2)}) async-start(), calls=%async_computation.1 | async-start | bytes 229376 | tf_op jit(solution)/shard_map/psum | solution.py:49
  26.3 106.5 %all-reduce.9.cloned.1.call-start = ((), (), s32[]{:S(2)}) async-start(), calls=%async_computation.2 | async-start | bytes 229376 | tf_op jit(solution)/shard_map/psum | solution.py:49
  79.3 22.0 %copy-start = (bf16[64,7168]{1,0:T(8,128)(2,1)S(1)}, bf16[64,7168]{1,0:T(8,128)(2,1)}, u32[]{:S(2)}) copy-start(bf16[64,7168]{1,0:T(8,128)(2,1)} %param.4) | copy-start | bytes 2752516
  101.2 105.1 %all-reduce.11.cloned.1.call-start = ((), (), s32[]{:S(2)}) async-start(), calls=%async_computation.3 | async-start | bytes 229376 | tf_op jit(solution)/shard_map/psum | solution.py:49
  184.2 245.2 %all-to-all-start = ((bf16[32,1,24,7168]{3,2,1,0:T(8,128)(2,1)}), bf16[32,1,24,7168]{3,2,1,0:T(8,128)(2,1)}, u32[]{:S(2)}, u32[]{:S(2)}) async-start(bf16[32,1,24,7168]{3,2,1,0:T(8,128)(2,1)} %bitcast.47), calls=%async_computation | async-start | bytes 22020096 | tf_op jit(solution)/shard_map/all_to_all | solution.py:65
  189.7 90.1 %all-reduce.13.cloned.1.call-start = ((), (), s32[]{:S(2)}) async-start(), calls=%async_computation.4 | async-start | bytes 229376 | tf_op jit(solution)/shard_map/psum | solution.py:49
  248.4 105.0 %all-reduce.15.cloned.1.call-start = ((), (), s32[]{:S(2)}) async-start(), calls=%async_computation.5 | async-start | bytes 229376 | tf_op jit(solution)/shard_map/psum | solution.py:49
Sparse Core Ops, SparseCore 0:
  26.4 32.6 all-reduce.6
  101.4 31.3 all-reduce.8
  174.9 31.3 all-reduce.10
  248.5 31.3 all-reduce.12
  322.0 31.3 all-reduce.14
where the time goes:
time: 467 us
  other arithmetic  210 us (45%)
  waiting for transfers between devices  194 us (42%)
  matrix products  30.9 us (7%)
  between operations  13.4 us (3%)
  local copies, waits for them, and re-layouts  12.6 us (3%)
  starting transfers between devices  5.86 us (1%)
    psum x5, waiting for transfers between devices, shards(): row_sums = lax.psum(partial_rows, 'hidden')  138 us
    reduce_sum x9, other arithmetic, row_terms(): return jnp.sum(values * values * cols_sq[:, None, :], axis=2)  104 us
    reduce_sum x5, other arithmetic, col_terms(): return jnp.sum(values * values * scale_sq[:, :, None], axis=1)  95.9 us
    all_to_all x1, waiting for transfers between devices, shards(): lax.all_to_all(outgoing, 'expert', split_axis=0, concat_axis=1, tiled=True)  55.9 us
    dot_general x1, matrix products, shards(): jnp.einsum('ensd,edf->ensf', routed, gate_eq, preferred_element_type=jnp....  15.9 us
    dot_general x1, matrix products, shards(): jnp.einsum('ensd,edf->ensf', routed, up_eq, preferred_element_type=jnp.fl...  15 us
    gather x1, local copies, waits for them, and re-layouts, shards(): outgoing = padded[slot_index.reshape(-1)].reshape(EXPERTS, 1, CAP, width)  9.4 us
  transfers between devices with their start and end apart: 6, of which 6 were waited for; matrix products, arithmetic and copies ran while one was open for 25% of the time, Pallas kernels for 0%

commit v1 on v0

v1 whole, which is shorter than its diff:
```python
import functools

import jax
import jax.numpy as jnp
from jax import lax
from jax.experimental import pallas as pl
from jax.experimental.pallas import tpu as pltpu
from jax.sharding import PartitionSpec as P

TOPK = 8
EXPERTS = 32
SWEEPS = 5
CAP = 24
EPS = 1e-06

F32 = jnp.float32
BF16 = jnp.bfloat16
NT = (((1,), (1,)), ((), ()))
BLOCK = 1792


def sweep_kernel(
    peers, gate_hbm, up_hbm, scale_ref, cols_ref, gate, up, mine, theirs, load_sem, send_sem, recv_sem
):
    experts, width, ff = gate.shape
    block = BLOCK if width % BLOCK == 0 else width
    blocks = width // block
    total_ff = ff * peers
    me = lax.axis_index("hidden")

    def load(e, i):
        src, dst = ((gate_hbm, gate), (up_hbm, up))[i]
        return pltpu.make_async_copy(src.at[e], dst.at[e], load_sem.at[e, i])

    for e in range(experts):
        load(e, 0).start()
        load(e, 1).start()

    barrier = pltpu.get_barrier_semaphore()
    for j in range(1, peers):
        pl.semaphore_signal(
            barrier,
            inc=1,
            device_id={"hidden": lax.rem(me + j, peers)},
            device_id_type=pl.DeviceIdType.MESH,
        )
    pl.semaphore_wait(barrier, peers - 1)

    def send(slot, e, j):
        return pltpu.make_async_remote_copy(
            src_ref=mine.at[slot, e],
            dst_ref=theirs.at[slot, e, j - 1],
            send_sem=send_sem.at[slot, e, j - 1],
            recv_sem=recv_sem.at[slot, e, j - 1],
            device_id={"hidden": lax.rem(me + j, peers)},
            device_id_type=pl.DeviceIdType.MESH,
        )

    ones = jnp.ones((16, 128), BF16)

    def rows(slot, e):
        gate_sq = cols_ref[e, 0] * cols_ref[e, 0]
        up_sq = cols_ref[e, 1] * cols_ref[e, 1]
        gate_sq, up_sq = gate_sq.astype(BF16), up_sq.astype(BF16)

        @pl.loop(0, blocks)
        def _(b):
            span = pl.ds(pl.multiple_of(b * block, block), block)
            parts = []
            for ref, cols in ((gate, gate_sq), (up, up_sq)):
                w = ref[e, span, :]
                w = w * w * cols
                parts += [w[:, i : i + 128] for i in range(0, ff, 128)]
            while len(parts) > 1:
                parts = [
                    parts[i] + parts[i + 1] if i + 1 < len(parts) else parts[i]
                    for i in range(0, len(parts), 2)
                ]
            sums = lax.dot_general(ones, parts[0], NT, preferred_element_type=F32)
            mine[slot, e, :, span] = sums[0:1]

        for j in range(1, peers):
            send(slot, e, j).start()

    def columns(slot, e):
        for j in range(1, peers):
            send(slot, e, j).wait()
        sums = mine[slot, e]
        for j in range(1, peers):
            sums = sums + theirs[slot, e, j - 1]
        scale = lax.rsqrt(width * sums / (2 * total_ff) + EPS)
        scale_ref[e] = scale

        def body(b, acc):
            span = pl.ds(pl.multiple_of(b * block, block), block)
            s = scale_ref[e, :, span]
            sq = jnp.broadcast_to(s * s, (16, block))
            high = sq.astype(BF16).astype(F32)
            row = lax.broadcasted_iota(jnp.int32, (16, block), 0)
            lhs = jnp.where(row == 0, high, jnp.where(row == 1, sq - high, 0.0)).astype(BF16)
            out = []
            for ref, total in ((gate, acc[0]), (up, acc[1])):
                w = ref[e, span, :]
                out.append(total + jnp.dot(lhs, w * w, preferred_element_type=F32))
            return tuple(out)

        zero = jnp.zeros((16, ff), F32)
        for i, total in enumerate(lax.fori_loop(0, blocks, body, (zero, zero))):
            cols_ref[e, i] = lax.rsqrt(total[0:1] + total[1:2] + EPS)

    cols_ref[...] = jnp.ones_like(cols_ref)

    @pl.loop(0, experts)
    def _(e):
        load(e, 0).wait()
        load(e, 1).wait()
        rows(0, e)

    @pl.loop(0, (SWEEPS - 1) * experts)
    def _(step):
        e = lax.rem(step, experts)
        slot = lax.rem(step // experts, 2)
        columns(slot, e)
        rows(1 - slot, e)

    @pl.loop(0, experts)
    def _(e):
        columns((SWEEPS - 1) % 2, e)


def sweeps(gate_weight, up_weight):
    experts, width, ff = gate_weight.shape
    peers = lax.axis_size("hidden")
    return pl.pallas_call(
        functools.partial(sweep_kernel, peers),
        out_shape=(
            jax.ShapeDtypeStruct((experts, 1, width), F32),
            jax.ShapeDtypeStruct((experts, 2, 1, ff), F32),
        ),
        in_specs=[pl.BlockSpec(memory_space=pltpu.HBM)] * 2,
        out_specs=(pl.BlockSpec(memory_space=pltpu.VMEM),) * 2,
        scratch_shapes=[
            pltpu.VMEM((experts, width, ff), BF16),
            pltpu.VMEM((experts, width, ff), BF16),
            pltpu.VMEM((2, experts, 1, width), F32),
            pltpu.VMEM((2, experts, peers - 1, 1, width), F32),
            pltpu.SemaphoreType.DMA((experts, 2)),
            pltpu.SemaphoreType.DMA((2, experts, peers - 1)),
            pltpu.SemaphoreType.DMA((2, experts, peers - 1)),
        ],
        compiler_params=pltpu.CompilerParams(
            collective_id=0, has_side_effects=True, vmem_limit_bytes=(64 << 20) - (256 << 10)
        ),
        cost_estimate=pl.CostEstimate(
            flops=4 * 10 * experts * width * ff,
            bytes_accessed=20 * experts * width * ff,
            transcendentals=0,
        ),
    )(gate_weight, up_weight)


def act_kernel(pick_ref, tokens_ref, scale_ref, cols_ref, gate_ref, up_ref, out_ref, acc):
    b, e = pl.program_id(0), pl.program_id(1)
    x = jnp.dot(pick_ref[e], tokens_ref[...], preferred_element_type=F32)
    x = (x * scale_ref[e]).astype(BF16)
    gate = jnp.dot(x, gate_ref[0], preferred_element_type=F32)
    up = jnp.dot(x, up_ref[0], preferred_element_type=F32)

    @pl.when(b == 0)
    def _():
        acc[e, 0] = gate
        acc[e, 1] = up

    @pl.when(b > 0)
    def _():
        acc[e, 0] += gate
        acc[e, 1] += up

    @pl.when(b == pl.num_programs(0) - 1)
    def _():
        g = acc[e, 0] * cols_ref[e, 0]
        u = acc[e, 1] * cols_ref[e, 1]
        out_ref[e] = (g / (1.0 + jnp.exp(-g)) * u).astype(BF16)


def activations(pick, tokens, scale, cols, gate_weight, up_weight):
    experts, width, ff = gate_weight.shape
    count, slots = tokens.shape[0], pick.shape[1]
    block = 1024 if width % 1024 == 0 else width
    whole = pl.BlockSpec(memory_space=pltpu.VMEM)
    weight = pl.BlockSpec((1, block, ff), lambda b, e: (e, b, 0))
    return pl.pallas_call(
        act_kernel,
        grid=(width // block, experts),
        out_shape=jax.ShapeDtypeStruct((experts, slots, ff), BF16),
        in_specs=[
            whole,
            pl.BlockSpec((count, block), lambda b, e: (0, b)),
            pl.BlockSpec((experts, 1, block), lambda b, e: (0, 0, b)),
            whole,
            weight,
            weight,
        ],
        out_specs=whole,
        scratch_shapes=[pltpu.VMEM((experts, 2, slots, ff), F32)],
        compiler_params=pltpu.CompilerParams(vmem_limit_bytes=48 << 20),
        cost_estimate=pl.CostEstimate(
            flops=4 * experts * slots * width * ff,
            bytes_accessed=4 * experts * width * ff,
            transcendentals=0,
        ),
    )(pick, tokens, scale, cols, gate_weight, up_weight)


def pick_table(expert_ids, first, experts, tok_local):
    sources = expert_ids.shape[0] // tok_local
    wanted = first + jnp.arange(experts, dtype=jnp.int32)
    named = jnp.any(expert_ids[None] == wanted[:, None, None], axis=2)
    named = named.reshape(experts, sources, tok_local)
    lower = jnp.arange(tok_local)[:, None] < jnp.arange(tok_local)[None, :]
    rank = jnp.dot(named.astype(BF16), lower.astype(BF16), preferred_element_type=F32)
    slot = jnp.where(named, rank.astype(jnp.int32), -1)
    slot = slot + jnp.arange(sources, dtype=jnp.int32)[None, :, None] * CAP
    slot = jnp.where(named, slot, -1).reshape(experts, 1, sources * tok_local)
    places = jnp.arange(sources * CAP, dtype=jnp.int32)[None, :, None]
    return (slot == places).astype(BF16)


def shards(tokens, expert_ids, gate_weight, up_weight):
    experts, width, ff = gate_weight.shape
    tok_local = tokens.shape[0]
    sources = lax.axis_size("expert")
    everyone = lax.all_gather(tokens, "expert", axis=0, tiled=True)
    scale, cols = sweeps(gate_weight, up_weight)
    pick = pick_table(expert_ids, lax.axis_index("expert") * experts, experts, tok_local)
    out = activations(pick, everyone, scale, cols, gate_weight, up_weight)
    return out.reshape(experts, sources, CAP, ff)


def solution(mesh):
    in_specs = (P("expert", None), P(), P("expert", None, "hidden"), P("expert", None, "hidden"))
    out_specs = P("expert", None, None, "hidden")
    return jax.shard_map(shards, mesh=mesh, in_specs=in_specs, out_specs=out_specs, check_vma=False)
```

time: 467 us -> 173 us (0.37)
  other arithmetic: 210 us -> 1.05 us
  waiting for transfers between devices: 194 us -> 0.73 us
  Pallas kernels: 0 us -> 155 us
  matrix products: 30.9 us -> 0.08 us
  local copies, waits for them, and re-layouts: 12.6 us -> 1.83 us
  starting transfers between devices: 5.86 us -> 0.01 us
    reduce_sum x15 -> x0, other arithmetic: 200 us -> none  [the longest x9 104 us: row_terms(): return jnp.sum(values * values * cols_sq[:, None, :], axis=2)]
    pallas_call x0 -> x2, Pallas kernels: none -> 155 us  [the longest x1 117 us: sweeps(): pl.pallas_call(functools.partial(sweep_kernel, peers), out_shape=(jax.Sha...]
    psum x5 -> x0, waiting for transfers between devices: 138 us -> none  [shards(): row_sums = lax.psum(partial_rows, 'hidden')]
    all_to_all x1 -> x0, waiting for transfers between devices: 55.9 us -> none  [shards(): lax.all_to_all(outgoing, 'expert', split_axis=0, concat_axis=1, tiled=True)]
    dot_general x2 -> x1, matrix products: 30.9 us -> 0.08 us  [pick_table(): jnp.dot(named.astype(BF16), lower.astype(BF16), preferred_element_type=F32)]
    gather x1 -> x0, local copies, waits for them, and re-layouts: 9.4 us -> none  [shards(): outgoing = padded[slot_index.reshape(-1)].reshape(EXPERTS, 1, CAP, width)]
    all_to_all x1 -> x0, starting transfers between devices: 5.51 us -> none  [shards(): lax.all_to_all(outgoing, 'expert', split_axis=0, concat_axis=1, tiled=True)]
  transfers between devices with their start and end apart: 6 -> 1, of which waited for: 6 -> 0; matrix products, arithmetic and copies ran while one was open for 25% -> 1% of each run, Pallas kernels for 0% -> 68%
where the time goes in v1:
time: 173 us
  Pallas kernels  155 us (90%)
  between operations  13.4 us (8%)
  local copies, waits for them, and re-layouts  1.83 us (1%)
    pallas_call x1, Pallas kernels, sweeps(): pl.pallas_call(functools.partial(sweep_kernel, peers), out_shape=(jax.Sha...  117 us
    pallas_call x1, Pallas kernels, activations(): pl.pallas_call(act_kernel, grid=(width // block, experts), out_shape=jax....  38.8 us
  transfers between devices with their start and end apart: 1, of which 0 were waited for; matrix products, arithmetic and copies ran while one was open for 1% of the time, Pallas kernels for 68%

profile of v1, /device:TPU:0, one launch (start us, length us, event | category | flops | bytes accessed | tf_op | source)
XLA Modules:
  0.0 172.5 jit_solution(6282745536090525962)
XLA Ops:
  6.5 0.0 all-gather.2.cloned.1.call-start
  6.5 0.7 all-gather.2.cloned.1.call-update
  7.3 0.8 compare_reduce_fusion
  8.1 0.1 reshape.18
  8.2 0.1 fusion.3
  8.3 0.1 eq.31
  8.4 116.6 %shard_map.46 = (f32[4,1,7168]{2,1,0:T(1,128)}, f32[4,2,1,512]{3,2,1,0:T(1,128)}) custom-call(bf16[4,7168,512]{2,1,0:T(8,128)(2,1)} %gate_ref.1, bf16[4,7168,512]{2,1,0:T(8,128)(2,1)} %up_ref.1), custom_call_target="tpu_custom_call" | custom-call | flops 587202560 | bytes 293601280 | tf_op jit(solution)/shard_map/pallas_call | solution.py:134
  125.0 0.2 fusion.pick_ref
  125.2 0.0 all-gather.2.cloned.1.call-done.tokens_ref
  125.2 0.0 copy-start
  125.2 0.9 copy-done
  126.1 0.0 copy-start.1
  126.1 0.7 copy-done.1
  126.8 38.8 %shard_map.47 = bf16[4,192,512]{2,1,0:T(8,128)(2,1)} custom-call(bf16[4,192,512]{2,1,0:T(8,128)(2,1)S(1)} %fusion.pick_ref, bf16[512,7168]{1,0:T(8,128)(2,1)} %all-gather.2.cloned.1.call-done.tokens_ref, f32[4,1,7168]{2,1,0:T(1,128)S(1)} %copy-done, f32[4,2,1,512]{3,2,1,0:T(1,128)S(1)} %copy-done.1, bf16[4,7168,512]{2,1,0:T(8,128)(2,1)} %gate_ref.1, ...), custom_call_target="tpu_custom_call" | custom-call | flops 11274289152 | bytes 58720256 | tf_op jit(solution)/shard_map/pallas_call | solution.py:192
  (2 shorter events, 0.0 us)
Async XLA Ops:
  6.5 118.7 %all-gather.2.cloned.1.call-start = ((), (), s32[]{:S(2)}) async-start(), calls=%async_computation | async-start | bytes 8257536 | tf_op jit(solution)/shard_map/all_gather | solution.py:233
  125.2 0.9 copy-start
  126.1 0.7 copy-start.1
Sparse Core Ops, SparseCore 0:
  9.5 114.8 all-gather.1

commit v2 on v1

--- a/solution.py
+++ b/solution.py
@@ -16,7 +16,7 @@
 F32 = jnp.float32
 BF16 = jnp.bfloat16
 NT = (((1,), (1,)), ((), ()))
-BLOCK = 1792
+BLOCK = 3584
 
 
 def sweep_kernel(
@@ -186,7 +186,7 @@
 def activations(pick, tokens, scale, cols, gate_weight, up_weight):
     experts, width, ff = gate_weight.shape
     count, slots = tokens.shape[0], pick.shape[1]
-    block = 1024 if width % 1024 == 0 else width
+    block = 1792 if width % 1792 == 0 else width
     whole = pl.BlockSpec(memory_space=pltpu.VMEM)
     weight = pl.BlockSpec((1, block, ff), lambda b, e: (e, b, 0))
     return pl.pallas_call(

time: 173 us -> 165 us (0.954)
  Pallas kernels: 155 us -> 140 us
  waiting for transfers between devices: 0.73 us -> 9.01 us
    pallas_call x1, Pallas kernels: 117 us -> 107 us  [sweeps(): pl.pallas_call(functools.partial(sweep_kernel, peers), out_shape=(jax.Sha...]
    all_gather x1, waiting for transfers between devices: 0.02 us -> 8.3 us  [shards(): everyone = lax.all_gather(tokens, 'expert', axis=0, tiled=True)]
    pallas_call x1, Pallas kernels: 38.8 us -> 32.2 us  [activations(): pl.pallas_call(act_kernel, grid=(width // block, experts), out_shape=jax....]
  transfers between devices with their start and end apart: 1 -> 1, of which waited for: 0 -> 1; matrix products, arithmetic and copies ran while one was open for 1% -> 1% of each run, Pallas kernels for 68% -> 65%
where the time goes in v2:
time: 165 us
  Pallas kernels  140 us (85%)
  between operations  13.4 us (8%)
  waiting for transfers between devices  9.01 us (5%)
  local copies, waits for them, and re-layouts  1.83 us (1%)
    pallas_call x1, Pallas kernels, sweeps(): pl.pallas_call(functools.partial(sweep_kernel, peers), out_shape=(jax.Sha...  107 us
    pallas_call x1, Pallas kernels, activations(): pl.pallas_call(act_kernel, grid=(width // block, experts), out_shape=jax....  32.2 us
    all_gather x1, waiting for transfers between devices, shards(): everyone = lax.all_gather(tokens, 'expert', axis=0, tiled=True)  8.3 us
  transfers between devices with their start and end apart: 1, of which 1 were waited for; matrix products, arithmetic and copies ran while one was open for 1% of the time, Pallas kernels for 65%

profile of v2, /device:TPU:0, one launch (start us, length us, event | category | flops | bytes accessed | tf_op | source)
XLA Modules:
  0.0 165.0 jit_solution(6831497756427699759)
XLA Ops:
  6.5 0.0 all-gather.2.cloned.1.call-start
  6.5 0.7 all-gather.2.cloned.1.call-update
  7.3 0.8 compare_reduce_fusion
  8.1 0.1 reshape.18
  8.2 0.1 fusion.3
  8.3 0.1 eq.31
  8.4 107.4 %shard_map.46 = (f32[4,1,7168]{2,1,0:T(1,128)}, f32[4,2,1,512]{3,2,1,0:T(1,128)}) custom-call(bf16[4,7168,512]{2,1,0:T(8,128)(2,1)} %gate_ref.1, bf16[4,7168,512]{2,1,0:T(8,128)(2,1)} %up_ref.1), custom_call_target="tpu_custom_call" | custom-call | flops 587202560 | bytes 293601280 | tf_op jit(solution)/shard_map/pallas_call | solution.py:134
  115.8 0.2 fusion.pick_ref
  116.1 8.3 %all-gather.2.cloned.1.call-done.tokens_ref = bf16[512,7168]{1,0:T(8,128)(2,1)} async-done(((bf16[64,7168]{1,0:T(8,128)(2,1)}), bf16[512,7168]{1,0:T(8,128)(2,1)}) %all-gather.2.cloned.1.call-update) | async-done | bytes 7340048 | tf_op jit(solution)/shard_map/all_gather | solution.py:233
  124.3 0.0 copy-start
  124.4 0.9 copy-done
  125.2 0.0 copy-start.1
  125.3 0.7 copy-done.1
  126.0 32.2 %shard_map.47 = bf16[4,192,512]{2,1,0:T(8,128)(2,1)} custom-call(bf16[4,192,512]{2,1,0:T(8,128)(2,1)S(1)} %fusion.pick_ref, bf16[512,7168]{1,0:T(8,128)(2,1)} %all-gather.2.cloned.1.call-done.tokens_ref, f32[4,1,7168]{2,1,0:T(1,128)S(1)} %copy-done, f32[4,2,1,512]{3,2,1,0:T(1,128)S(1)} %copy-done.1, bf16[4,7168,512]{2,1,0:T(8,128)(2,1)} %gate_ref.1, ...), custom_call_target="tpu_custom_call" | custom-call | flops 11274289152 | bytes 58720256 | tf_op jit(solution)/shard_map/pallas_call | solution.py:192
  (2 shorter events, 0.0 us)
Async XLA Ops:
  6.5 117.8 %all-gather.2.cloned.1.call-start = ((), (), s32[]{:S(2)}) async-start(), calls=%async_computation | async-start | bytes 8257536 | tf_op jit(solution)/shard_map/all_gather | solution.py:233
  124.3 0.9 copy-start
  125.2 0.7 copy-start.1
Sparse Core Ops, SparseCore 0:
  9.5 114.7 all-gather.1
